TPU v7x, 32 devices: a whole 2x2x4 slice. The times are simulated.
32 devices in a mesh: groups: 1, seq: 32 (over z, y, x, core), fsdp: 1.
Axes of the slice: x: 2, y: 2, z: 4, core: 2. Of those that a mesh axis runs over, the one named last changes fastest.
Arguments:
- fine: bfloat16 [4096, 1024], P(('groups', 'seq'), 'fsdp'), may hold values from -3 to 3
- queries: bfloat16 [4096, 1024], P(('groups', 'seq'), 'fsdp'), may hold values from -180 to 180
- keys: bfloat16 [512, 1024], P(('groups', 'seq'), 'fsdp'), may hold values from -6 to 6
- values: bfloat16 [512, 1024], P(('groups', 'seq'), 'fsdp'), may hold values from -24 to 24
- pattern: int32 [32, 2], P(('groups', 'seq')), may hold values from 0 to 3, as said below
- counts: int32 [32], P(('groups', 'seq')), may hold values from 1 to 2, as said below
- norm_gain: float32 [1024], replicated, may hold values from 0.1 to 1.9
- w_in: bfloat16 [1024, 2048], P('fsdp'), may hold values from -0.1875 to 0.1875
- w_out: bfloat16 [2048, 1024], P('fsdp'), may hold values from -0.125 to 0.125
Outputs:
- mixed: bfloat16 [4096, 1024], P(('groups', 'seq', 'fsdp'))
Inputs may be any that keep to these rules, and one draw needn't show every extreme that they name: `pattern`: the 2 entries of a row are different key blocks; the first is the block that holds coarse row (b * 128) // 8 for query block b. The query blocks of one index of seq have counts that differ by at most one; on some index of seq every query block has 2.
All inputs are finite; a program needn't handle non-finite values.
Results may differ from a plain program's by a relative error of at most 0.0065.
Values may be sent and summed in bfloat16 or wider, within the bound.
A program may use at most 64 MiB of HBM per device.

v0:
```python
import math

import jax
import jax.numpy as jnp
from jax import lax
from jax.sharding import PartitionSpec as P

HEAD = 64
QBLK = 128
KBLK = 128


def shards(fine, queries, keys, values, pattern, counts, norm_gain, w_in, w_out):
    local_rows, half_width = queries.shape
    head_count = half_width // HEAD
    scale_factor = 1.0 / math.sqrt(HEAD)
    query_heads = queries.reshape(local_rows, head_count, HEAD)
    slot_count = pattern.shape[1]
    block_total = keys.shape[0] * lax.axis_size("seq") // KBLK
    slot_live = jnp.arange(slot_count, dtype=jnp.int32)[None, :] < counts[:, None]
    block_ids = jnp.arange(block_total, dtype=jnp.int32)
    chosen = jnp.any(
        (pattern[:, :, None] == block_ids[None, None, :]) & slot_live[:, :, None], axis=1
    )

    def absorb(running, key_rows, value_rows, first_row):
        width = key_rows.shape[0]
        row_block = (first_row + jnp.arange(width, dtype=jnp.int32)) // KBLK
        allowed = jnp.any(
            chosen[:, None, :] & (row_block[:, None] == block_ids[None, :])[None, :, :], axis=2
        )
        allowed = jnp.repeat(allowed, QBLK, axis=0)[None, :, :]
        maxima, totals, weighted = running
        scores = (
            jnp.einsum(
                "qhd,khd->hqk",
                query_heads,
                key_rows.reshape(width, head_count, HEAD),
                preferred_element_type=jnp.float32,
            )
            * scale_factor
        )
        piece_max = jnp.max(jnp.where(allowed, scores, -1e30), axis=2)
        new_max = jnp.maximum(maxima, piece_max)
        probs = jnp.where(
            allowed, jnp.exp(jnp.where(allowed, scores - new_max[:, :, None], -1e30)), 0.0
        )
        factor = jnp.exp(maxima - new_max)
        totals = totals * factor + jnp.sum(probs, axis=2)
        update = jnp.einsum(
            "hqk,khd->qhd",
            probs.astype(jnp.bfloat16),
            value_rows.reshape(width, head_count, HEAD),
            preferred_element_type=jnp.float32,
        )
        weighted = weighted * jnp.transpose(factor)[:, :, None] + update
        return (new_max, totals, weighted)

    initial = (
        jnp.full((head_count, local_rows), -1e30, jnp.float32),
        jnp.zeros((head_count, local_rows), jnp.float32),
        jnp.zeros((local_rows, head_count, HEAD), jnp.float32),
    )
    key_piece = lax.all_gather(keys, "seq", axis=0, tiled=True)
    value_piece = lax.all_gather(values, "seq", axis=0, tiled=True)
    width = key_piece.shape[0]
    span = 512

    def inner(turn, state):
        offset = turn * span
        return absorb(
            state,
            lax.dynamic_slice_in_dim(key_piece, offset, span, 0),
            lax.dynamic_slice_in_dim(value_piece, offset, span, 0),
            offset,
        )

    maxima, totals, weighted = lax.fori_loop(0, width // span, inner, initial)
    attn = (
        (weighted / jnp.transpose(totals)[:, :, None])
        .astype(jnp.bfloat16)
        .reshape(local_rows, half_width)
    )
    moved_fine, moved_attn = (
        lax.all_to_all(fine, "fsdp", split_axis=0, concat_axis=1, tiled=True),
        lax.all_to_all(attn, "fsdp", split_axis=0, concat_axis=1, tiled=True),
    )
    middle = moved_fine.astype(jnp.float32) + moved_attn.astype(jnp.float32)
    mean_square = jnp.mean(middle * middle, axis=1, keepdims=True)
    normed = (middle * lax.rsqrt(mean_square + 1e-06) * norm_gain).astype(jnp.bfloat16)
    before = jnp.dot(
        normed, lax.all_gather(w_in, "fsdp", axis=0, tiled=True), preferred_element_type=jnp.float32
    )
    hidden = jax.nn.gelu(before, approximate=True).astype(jnp.bfloat16)
    output_sum = jnp.dot(
        hidden,
        lax.all_gather(w_out, "fsdp", axis=0, tiled=True),
        preferred_element_type=jnp.float32,
    )
    return (middle + output_sum).astype(jnp.bfloat16)


def solution(mesh):
    return jax.shard_map(
        shards,
        mesh=mesh,
        in_specs=(
            P(("groups", "seq"), "fsdp"),
            P(("groups", "seq"), "fsdp"),
            P(("groups", "seq"), "fsdp"),
            P(("groups", "seq"), "fsdp"),
            P(("groups", "seq"), None),
            P(("groups", "seq")),
            P(),
            P("fsdp", None),
            P("fsdp", None),
        ),
        out_specs=P(("groups", "seq", "fsdp"), None),
        check_vma=False,
    )
```

profile of v0, /device:TPU:1, one launch (start us, length us, event | category | flops | bytes accessed | tf_op | source)
XLA Modules:
  0.0 140.0 jit_solution(5598994097227791347)
XLA Ops:
  6.5 0.0 all-gather.3.cloned.1.call-start
  6.5 0.7 all-gather.3.cloned.1.call-update
  7.3 0.0 all-gather.5.cloned.1.call-start
  7.3 0.7 all-gather.5.cloned.1.call-update
  8.7 1.1 copy.18
  9.8 0.7 and_reduce_fusion
  10.6 0.1 fusion.37
  10.6 55.8 %all-gather.3.cloned.1.call-done = bf16[512,1024]{1,0:T(8,128)(2,1)} async-done(((bf16[16,1024]{1,0:T(8,128)(2,1)}), bf16[512,1024]{1,0:T(8,128)(2,1)}) %all-gather.3.cloned.1.call-update) | async-done | bytes 1048592 | tf_op jit(solution)/shard_map/all_gather | solution.py:64
  66.4 1.5 %copy.19 = bf16[512,1024]{0,1:T(8,128)(2,1)S(1)} copy(bf16[512,1024]{1,0:T(8,128)(2,1)} %all-gather.3.cloned.1.call-done) | data formatting | bytes 2097152 | tf_op jit(solution)/shard_map/all_gather | solution.py:64
  67.9 0.8 select_reduce_fusion
  68.8 0.0 copy-start
  68.8 1.9 %copy-done = f32[16,128,512]{2,1,0:T(8,128)} copy-done((f32[16,128,512]{2,1,0:T(8,128)}, f32[16,128,512]{2,1,0:T(8,128)S(1)}, u32[]{:S(2)}) %copy-start) | copy-done | bytes 4194328
  70.7 1.2 fusion
  71.9 50.1 %all-gather.5.cloned.1.call-done = bf16[512,1024]{1,0:T(8,128)(2,1)} async-done(((bf16[16,1024]{1,0:T(8,128)(2,1)}), bf16[512,1024]{1,0:T(8,128)(2,1)}) %all-gather.5.cloned.1.call-update) | async-done | bytes 1048592 | tf_op jit(solution)/shard_map/all_gather | solution.py:65
  122.0 1.5 %copy.20 = bf16[512,1024]{0,1:T(8,128)(2,1)S(1)} copy(bf16[512,1024]{1,0:T(8,128)(2,1)} %all-gather.5.cloned.1.call-done) | data formatting | bytes 2097152 | tf_op jit(solution)/shard_map/all_gather | solution.py:65
  123.5 0.0 copy-start.1
  123.5 0.0 copy-start.2
  123.5 3.4 %fusion.23 = bf16[128,16,64]{0,2,1:T(8,128)(2,1)S(1)} fusion(bf16[512,16,64]{0,2,1:T(8,128)(2,1)S(1)} %bitcast.30, f32[16,128,512]{2,1,0:T(8,128)} %copy-done, f32[16,128]{1,0:T(8,128)S(1)} %get-tuple-element.24, pred[512]{0:T(512)(128)(4,1)S(1)} %fusion.37, f32[128,16]{0,1:T(8,128)S(1)} %bitcast_add_fusion, f32[128,16]{0,1:T(8,128)S(1)} %get-tuple-element.23), kind=kOutput, calls=%fused_computation.20 | convolution fusion | flops 139853824 | bytes 5530112 | tf_op jit(solution)/shard_map/while/body/eval_jaxpr/hqk,khd->qhd/dot_general | solution.py:50
  126.9 0.1 bitcast_convert_fusion
  127.0 0.2 copy.21
  127.2 0.0 copy-done.1
  127.2 0.2 multiply_reduce_fusion
  127.3 0.0 copy-done.2
  127.4 5.8 %fusion.11 = bf16[128,1024]{1,0:T(8,128)(2,1)} fusion(bf16[2048,1024]{1,0:T(8,128)(2,1)} %param.17, bf16[1024,2048]{1,0:T(8,128)(2,1)} %param.16, f32[128,1024]{1,0:T(8,128)S(1)} %copy.21, bf16[128,1024]{1,0:T(8,128)(2,1)S(1)} %copy-done.1, f32[1024]{0:T(1024)S(1)} %copy-done.2, f32[128]{0:T(128)S(1)} %add_rsqrt_fusion), kind=kOutput, calls=%fused_computation.10 | convolution fusion | flops 1077280768 | bytes 9441792 | tf_op jit(solution)/shard_map/dot_general | solution.py:95
  (5 shorter events, 0.0 us)
Async XLA Ops:
  6.5 59.9 %all-gather.3.cloned.1.call-start = ((), (), s32[]{:S(2)}) async-start(), calls=%async_computation | async-start | bytes 1081344 | tf_op jit(solution)/shard_map/all_gather | solution.py:64
  7.3 114.7 %all-gather.5.cloned.1.call-start = ((), (), s32[]{:S(2)}) async-start(), calls=%async_computation.1 | async-start | bytes 1081344 | tf_op jit(solution)/shard_map/all_gather | solution.py:65
  68.8 1.9 %copy-start = (f32[16,128,512]{2,1,0:T(8,128)}, f32[16,128,512]{2,1,0:T(8,128)S(1)}, u32[]{:S(2)}) copy-start(f32[16,128,512]{2,1,0:T(8,128)S(1)} %get-tuple-element.26) | copy-start | bytes 12582916
  123.5 3.7 %copy-start.1 = (bf16[128,1024]{1,0:T(8,128)(2,1)S(1)}, bf16[128,1024]{1,0:T(8,128)(2,1)}, u32[]{:S(2)}) copy-start(bf16[128,1024]{1,0:T(8,128)(2,1)} %param.9) | copy-start | bytes 786436
  123.5 3.9 %copy-start.2 = (f32[1024]{0:T(1024)S(1)}, f32[1024]{0:T(1024)}, u32[]{:S(2)}) copy-start(f32[1024]{0:T(1024)} %param.15) | copy-start | bytes 12292
Sparse Core Ops, SparseCore 0:
  10.2 56.1 all-gather.2
  69.3 52.6 all-gather.4
where the time goes:
time: 140 us
  waiting for transfers between devices  107 us (76%)
  between operations  14.2 us (10%)
  matrix products  10.1 us (7%)
  local copies, waits for them, and re-layouts  6.22 us (4%)
  other arithmetic  2.24 us (2%)
    all_gather x1, waiting for transfers between devices, shards(): key_piece = lax.all_gather(keys, 'seq', axis=0, tiled=True)  55.8 us
    all_gather x1, waiting for transfers between devices, shards(): value_piece = lax.all_gather(values, 'seq', axis=0, tiled=True)  50.1 us
    dot_general x1, matrix products, shards(): jnp.dot(hidden, lax.all_gather(w_out, 'fsdp', axis=0, tiled=True), prefer...  5.83 us
    dot_general x1, matrix products, absorb(): jnp.einsum('hqk,khd->qhd', probs.astype(jnp.bfloat16), value_rows.reshape...  3.43 us
    unnamed x7, local copies, waits for them, and re-layouts  3.04 us
  transfers between devices with their start and end apart: 2, of which 2 were waited for; matrix products, arithmetic and copies ran while one was open for 4% of the time, Pallas kernels for 0%

commit v1 on v0

--- a/solution.py
+++ b/solution.py
@@ -1,13 +1,217 @@
+import functools
 import math
 
 import jax
 import jax.numpy as jnp
 from jax import lax
+from jax.experimental import pallas as pl
+from jax.experimental.pallas import tpu as pltpu
 from jax.sharding import PartitionSpec as P
 
 HEAD = 64
 QBLK = 128
 KBLK = 128
+MESH = pl.DeviceIdType.MESH
+PLANE = 8
+LEVELS = 4
+
+
+def choose(ref, others, picks, columns):
+    block = None
+    for start, pick in zip(others, picks):
+        part = ref[pl.ds(start, KBLK), columns] * pick
+        block = part if block is None else block + part
+    return block
+
+
+def attend_pair(q_ref, k_ref, v_ref, fine_ref, mid_ref, own, others, picks, bias, pair):
+    columns = pl.ds(pair * 2 * HEAD, 2 * HEAD)
+    q = q_ref[:, columns] * jnp.bfloat16(1.0 / math.sqrt(HEAD))
+    lane = lax.broadcasted_iota(jnp.int32, q.shape, 1)
+    zero = jnp.zeros_like(q)
+    both = jnp.concatenate([jnp.where(lane < HEAD, q, zero), jnp.where(lane < HEAD, zero, q)], axis=0)
+    k = jnp.concatenate([k_ref[pl.ds(own, KBLK), columns], choose(k_ref, others, picks, columns)], axis=0)
+    s = lax.dot_general(both, k, (((1,), (1,)), ((), ())), preferred_element_type=jnp.float32) + bias
+    top = jnp.max(s, axis=1, keepdims=True)
+    weights = jnp.exp(s - top).astype(jnp.bfloat16)
+    v = jnp.concatenate([v_ref[pl.ds(own, KBLK), columns], choose(v_ref, others, picks, columns)], axis=0)
+    v = jnp.concatenate([v, jnp.ones_like(v)], axis=1)
+    summed = jnp.dot(weights, v, preferred_element_type=jnp.float32)
+    out = summed[:, : 2 * HEAD] / summed[:, 2 * HEAD :]
+    rows = q.shape[0]
+    out = jnp.where(lane < HEAD, out[:rows], out[rows:]).astype(jnp.bfloat16)
+    mid_ref[:, columns] = fine_ref[:, columns].astype(jnp.float32) + out.astype(jnp.float32)
+
+
+def feed_forward(mid_ref, gain_ref, win, wout, hid_ref, out_ref, wait_in, wait_out):
+    mid = mid_ref[...]
+    mean_square = jnp.mean(mid * mid, axis=1, keepdims=True)
+    normed = (mid * lax.rsqrt(mean_square + 1e-06) * gain_ref[...]).astype(jnp.bfloat16)
+    wait_in()
+    step = 256
+    for c in range(hid_ref.shape[1] // step):
+        cols = pl.ds(c * step, step)
+        before = jnp.dot(normed, win[:, cols], preferred_element_type=jnp.float32)
+        hid_ref[:, cols] = jax.nn.gelu(before, approximate=True).astype(jnp.bfloat16)
+    wait_out()
+    for c in range(out_ref.shape[1] // step):
+        cols = pl.ds(c * step, step)
+        y = jnp.dot(hid_ref[...], wout[:, cols], preferred_element_type=jnp.float32)
+        out_ref[:, cols] = (mid_ref[:, cols] + y).astype(jnp.bfloat16)
+
+
+def kernel(
+    pattern_hbm, counts_hbm, q_hbm, k_ref, v_ref, fine_hbm, gain_hbm, win_hbm, wout_hbm,
+    out_ref,
+    pattern_ref, counts_ref, q_ref, fine_ref, gain_ref, kg, vg, win, wout, mid, hid, load_sem, send_sem, recv_sem,
+):
+    me = lax.axis_index("seq")
+    shard = k_ref.shape[0]
+    z, y, x, c = me // PLANE, (me // 4) % 2, (me // 2) % 2, me % 2
+
+    def at(zz, yy, xx, cc):
+        return zz * PLANE + yy * 4 + xx * 2 + cc
+
+    zs = [(z + d) % LEVELS for d in (0, 1, 3, 2)]
+    x_nbr, y_nbr, core = at(z, y, 1 - x, c), at(z, 1 - y, x, c), at(z, y, x, 1 - c)
+    z_nbrs = [at(zz, y, x, c) for zz in zs[1:]]
+
+    barrier = pltpu.get_barrier_semaphore()
+    greeted = [x_nbr, y_nbr, core] + z_nbrs
+    for other in greeted:
+        pl.semaphore_signal(barrier, inc=1, device_id={"seq": other}, device_id_type=MESH)
+    own_rows = pl.ds(pl.multiple_of(me * shard, shard), shard)
+    moves = [
+        (k_ref, kg.at[own_rows, :]), (v_ref, vg.at[own_rows, :]), (q_hbm, q_ref), (pattern_hbm, pattern_ref),
+        (counts_hbm, counts_ref), (fine_hbm, fine_ref), (gain_hbm, gain_ref), (win_hbm, win), (wout_hbm, wout),
+    ]
+    loads = [pltpu.make_async_copy(a, b, load_sem.at[i]) for i, (a, b) in enumerate(moves)]
+    for load in loads:
+        load.start()
+    pl.semaphore_wait(barrier, len(greeted))
+
+    gathered = (kg, vg)
+    sent = []
+
+    def rows_of(origin):
+        return pl.ds(pl.multiple_of(origin * shard, shard), shard)
+
+    def copy_of(kind, origin, target, own=False):
+        place = gathered[kind].at[rows_of(origin), :]
+        source = (k_ref, v_ref)[kind] if own else place
+        return pltpu.make_async_remote_copy(
+            src_ref=source, dst_ref=place,
+            send_sem=send_sem.at[len(sent)], recv_sem=recv_sem.at[kind, origin],
+            device_id={"seq": target}, device_id_type=MESH,
+        )
+
+    def send(kind, origin, target, own=False):
+        copy = copy_of(kind, origin, target, own)
+        copy.start()
+        sent.append(copy)
+
+    def arrive(kind, origin):
+        pltpu.make_async_remote_copy(
+            src_ref=gathered[kind].at[rows_of(origin), :], dst_ref=gathered[kind].at[rows_of(origin), :],
+            send_sem=send_sem.at[0], recv_sem=recv_sem.at[kind, origin],
+            device_id={"seq": core}, device_id_type=MESH,
+        ).wait_recv()
+
+    def column(level):
+        origin = at(zs[level], y, x, c)
+        own = level == 0
+        for kind in (0, 1):
+            if not own:
+                arrive(kind, origin)
+            for target in (x_nbr, y_nbr, core):
+                send(kind, origin, target, own)
+
+    def beside(level):
+        by_y, by_x = at(zs[level], 1 - y, x, c), at(zs[level], y, 1 - x, c)
+        arrive(0, by_y)
+        send(0, by_y, x_nbr)
+        send(0, by_y, core)
+        arrive(0, by_x)
+        send(0, by_x, core)
+        arrive(1, by_x)
+        send(1, by_x, y_nbr)
+        send(1, by_x, core)
+        arrive(1, by_y)
+        send(1, by_y, core)
+
+    def across(level):
+        origin = at(zs[level], 1 - y, 1 - x, c)
+        for kind in (0, 1):
+            arrive(kind, origin)
+            send(kind, origin, core)
+
+    for kind in (0, 1):
+        for target in z_nbrs:
+            send(kind, me, target, True)
+    for turn in range(LEVELS + 2):
+        if turn < LEVELS:
+            column(turn)
+        if 0 <= turn - 1 < LEVELS:
+            beside(turn - 1)
+        if 0 <= turn - 2 < LEVELS:
+            across(turn - 2)
+    for zz in zs:
+        for yy in (y, 1 - y):
+            for xx in (x, 1 - x):
+                for kind in (0, 1):
+                    arrive(kind, at(zz, yy, xx, 1 - c))
+
+    for load in loads[:6]:
+        load.wait()
+    own = pl.multiple_of(z * KBLK, KBLK)
+    others = [pl.multiple_of(zz * KBLK, KBLK) for zz in zs[1:]]
+    second = jnp.broadcast_to(pattern_ref[:, 1:2], (1, 2 * HEAD))
+    picks = [jnp.where(second == zz, 1.0, 0.0).astype(jnp.bfloat16) for zz in zs[1:]]
+    used = jnp.broadcast_to(counts_ref[...], (1, KBLK))
+    bias = jnp.concatenate([jnp.zeros((1, KBLK), jnp.float32), jnp.where(used > 1, 0.0, -1e30)], axis=1)
+    for pair in range(q_ref.shape[1] // (2 * HEAD)):
+        attend_pair(q_ref, kg, vg, fine_ref, mid, own, others, picks, bias, pair)
+    loads[6].wait()
+    feed_forward(mid, gain_ref, win, wout, hid, out_ref, loads[7].wait, loads[8].wait)
+    for copy in sent:
+        copy.wait_send()
+
+
+def fast_shards(fine, queries, keys, values, pattern, counts, norm_gain, w_in, w_out):
+    rows, width = fine.shape
+    hidden = w_in.shape[1]
+    gathered = (keys.shape[0] * lax.axis_size("seq"), width)
+    vmem = pl.BlockSpec(memory_space=pltpu.VMEM)
+    hbm = pl.BlockSpec(memory_space=pl.ANY)
+    sends = 6 + LEVELS * (6 + 6 + 2)
+    return pl.pallas_call(
+        kernel,
+        out_shape=jax.ShapeDtypeStruct((rows, width), jnp.bfloat16),
+        in_specs=[hbm] * 9,
+        out_specs=vmem,
+        scratch_shapes=[
+            pltpu.VMEM(pattern.shape, jnp.int32),
+            pltpu.VMEM((1, 1), jnp.int32),
+            pltpu.VMEM(queries.shape, jnp.bfloat16),
+            pltpu.VMEM(fine.shape, jnp.bfloat16),
+            pltpu.VMEM((1, width), jnp.float32),
+            pltpu.VMEM(gathered, jnp.bfloat16),
+            pltpu.VMEM(gathered, jnp.bfloat16),
+            pltpu.VMEM(w_in.shape, jnp.bfloat16),
+            pltpu.VMEM(w_out.shape, jnp.bfloat16),
+            pltpu.VMEM((rows, width), jnp.float32),
+            pltpu.VMEM((rows, hidden), jnp.bfloat16),
+            pltpu.SemaphoreType.DMA((9,)),
+            pltpu.SemaphoreType.DMA((sends,)),
+            pltpu.SemaphoreType.DMA((2, gathered[0] // keys.shape[0])),
+        ],
+        compiler_params=pltpu.CompilerParams(
+            collective_id=0, has_side_effects=True, vmem_limit_bytes=58 * 2**20
+        ),
+        cost_estimate=pl.CostEstimate(
+            flops=4 * rows * width * hidden, bytes_accessed=4 * width * hidden, transcendentals=rows * hidden
+        ),
+    )(pattern, counts.reshape(1, 1), queries, keys, values, fine, norm_gain.reshape(1, -1), w_in, w_out)
 
 
 def shards(fine, queries, keys, values, pattern, counts, norm_gain, w_in, w_out):
@@ -99,10 +303,13 @@
     )
     return (middle + output_sum).astype(jnp.bfloat16)
 
+def is_small(mesh):
+    return mesh.shape["groups"] == 1 and mesh.shape["fsdp"] == 1 and mesh.shape["seq"] == PLANE * LEVELS
+
 
 def solution(mesh):
     return jax.shard_map(
-        shards,
+        fast_shards if is_small(mesh) else shards,
         mesh=mesh,
         in_specs=(
             P(("groups", "seq"), "fsdp"),

time: 140 us -> 28.4 us (0.20)
  waiting for transfers between devices: 107 us -> 0 us
  Pallas kernels: 0 us -> 25.9 us
  between operations: 14.2 us -> 0.66 us
  matrix products: 10.1 us -> 0 us
  local copies, waits for them, and re-layouts: 6.22 us -> 1.67 us
  other arithmetic: 2.24 us -> 0 us
    all_gather x2 -> x0, waiting for transfers between devices: 106 us -> none  [the longest x1 55.8 us: shards(): key_piece = lax.all_gather(keys, 'seq', axis=0, tiled=True)]
    pallas_call x0 -> x1, Pallas kernels: none -> 25.9 us  [fast_shards(): pl.pallas_call(kernel, out_shape=jax.ShapeDtypeStruct((rows, width), jnp....]
    dot_general x3 -> x0, matrix products: 10.1 us -> none  [the longest x1 5.83 us: shards(): jnp.dot(hidden, lax.all_gather(w_out, 'fsdp', axis=0, tiled=True), prefer...]
    all_gather x2 -> x0, local copies, waits for them, and re-layouts: 2.98 us -> none  [the longest x1 1.49 us: shards(): key_piece = lax.all_gather(keys, 'seq', axis=0, tiled=True)]
    unnamed x2 -> x0, waiting for transfers between devices: 1.41 us -> none
    unnamed x7 -> x1, local copies, waits for them, and re-layouts: 3.04 us -> 1.67 us
  transfers between devices with their start and end apart: 2 -> 0, of which waited for: 2 -> 0; matrix products, arithmetic and copies ran while one was open for 4% -> 0% of each run, Pallas kernels for 0% -> 0%
where the time goes in v1:
time: 28.4 us; the launch traced here: 28.3 us
  Pallas kernels  25.9 us (91%)
  local copies, waits for them, and re-layouts  1.67 us (6%)
  between operations  0.66 us (2%)
    pallas_call x1, Pallas kernels, fast_shards(): pl.pallas_call(kernel, out_shape=jax.ShapeDtypeStruct((rows, width), jnp....  25.9 us
    unnamed x1, local copies, waits for them, and re-layouts  1.67 us

profile of v1, /device:TPU:1, one launch (start us, length us, event | category | flops | bytes accessed | tf_op | source)
XLA Modules:
  0.0 28.3 jit_solution(13035173507281253164)
XLA Ops:
  0.7 25.9 %shard_map.91 = bf16[128,1024]{1,0:T(8,128)(2,1)} custom-call(s32[1,2]{1,0:T(1,128)} %pattern_hbm.1, s32[1,1]{1,0:T(1,128)} %bitcast.2.counts_hbm, bf16[128,1024]{1,0:T(8,128)(2,1)} %q_hbm.1, bf16[16,1024]{1,0:T(8,128)(2,1)} %k_ref.1, bf16[16,1024]{1,0:T(8,128)(2,1)} %v_ref.1, bf16[128,1024]{1,0:T(8,128)(2,1)} %fine_hbm.1, f32[1,1024]{1,0:T(1,128)} %bitcast.3, ...), custom_call_target="tpu_custom_call" | custom-call | flops 1073741824 | bytes 8388608 | tf_op jit(solution)/shard_map/pallas_call | solution.py:187
  26.6 1.7 %copy.12 = bf16[128,1024]{1,0:T(8,128)(2,1)} copy(bf16[128,1024]{1,0:T(8,128)(2,1)} %shard_map.91) | data formatting | bytes 524288

commit v2 on v1

--- a/solution.py
+++ b/solution.py
@@ -24,7 +24,7 @@
     return block
 
 
-def attend_pair(q_ref, k_ref, v_ref, fine_ref, mid_ref, own, others, picks, bias, pair):
+def weigh_pair(q_ref, k_ref, weight_ref, own, others, picks, bias, pair):
     columns = pl.ds(pair * 2 * HEAD, 2 * HEAD)
     q = q_ref[:, columns] * jnp.bfloat16(1.0 / math.sqrt(HEAD))
     lane = lax.broadcasted_iota(jnp.int32, q.shape, 1)
@@ -33,12 +33,18 @@
     k = jnp.concatenate([k_ref[pl.ds(own, KBLK), columns], choose(k_ref, others, picks, columns)], axis=0)
     s = lax.dot_general(both, k, (((1,), (1,)), ((), ())), preferred_element_type=jnp.float32) + bias
     top = jnp.max(s, axis=1, keepdims=True)
-    weights = jnp.exp(s - top).astype(jnp.bfloat16)
+    weight_ref[pair] = jnp.exp(s - top).astype(jnp.bfloat16)
+
+
+def attend_pair(weight_ref, v_ref, fine_ref, mid_ref, own, others, picks, pair):
+    columns = pl.ds(pair * 2 * HEAD, 2 * HEAD)
+    weights = weight_ref[pair]
     v = jnp.concatenate([v_ref[pl.ds(own, KBLK), columns], choose(v_ref, others, picks, columns)], axis=0)
     v = jnp.concatenate([v, jnp.ones_like(v)], axis=1)
     summed = jnp.dot(weights, v, preferred_element_type=jnp.float32)
     out = summed[:, : 2 * HEAD] / summed[:, 2 * HEAD :]
-    rows = q.shape[0]
+    rows = fine_ref.shape[0]
+    lane = lax.broadcasted_iota(jnp.int32, (rows, 2 * HEAD), 1)
     out = jnp.where(lane < HEAD, out[:rows], out[rows:]).astype(jnp.bfloat16)
     mid_ref[:, columns] = fine_ref[:, columns].astype(jnp.float32) + out.astype(jnp.float32)
 
@@ -63,7 +69,7 @@
 def kernel(
     pattern_hbm, counts_hbm, q_hbm, k_ref, v_ref, fine_hbm, gain_hbm, win_hbm, wout_hbm,
     out_ref,
-    pattern_ref, counts_ref, q_ref, fine_ref, gain_ref, kg, vg, win, wout, mid, hid, load_sem, send_sem, recv_sem,
+    pattern_ref, counts_ref, q_ref, fine_ref, gain_ref, kg, vg, win, wout, mid, hid, weights, load_sem, send_sem, recv_sem,
 ):
     me = lax.axis_index("seq")
     shard = k_ref.shape[0]
@@ -155,12 +161,13 @@
             beside(turn - 1)
         if 0 <= turn - 2 < LEVELS:
             across(turn - 2)
-    for zz in zs:
-        for yy in (y, 1 - y):
-            for xx in (x, 1 - x):
-                for kind in (0, 1):
+    def arrive_core(kind):
+        for zz in zs:
+            for yy in (y, 1 - y):
+                for xx in (x, 1 - x):
                     arrive(kind, at(zz, yy, xx, 1 - c))
 
+    arrive_core(0)
     for load in loads[:6]:
         load.wait()
     own = pl.multiple_of(z * KBLK, KBLK)
@@ -170,7 +177,10 @@
     used = jnp.broadcast_to(counts_ref[...], (1, KBLK))
     bias = jnp.concatenate([jnp.zeros((1, KBLK), jnp.float32), jnp.where(used > 1, 0.0, -1e30)], axis=1)
     for pair in range(q_ref.shape[1] // (2 * HEAD)):
-        attend_pair(q_ref, kg, vg, fine_ref, mid, own, others, picks, bias, pair)
+        weigh_pair(q_ref, kg, weights, own, others, picks, bias, pair)
+    arrive_core(1)
+    for pair in range(q_ref.shape[1] // (2 * HEAD)):
+        attend_pair(weights, vg, fine_ref, mid, own, others, picks, pair)
     loads[6].wait()
     feed_forward(mid, gain_ref, win, wout, hid, out_ref, loads[7].wait, loads[8].wait)
     for copy in sent:
@@ -201,6 +211,7 @@
             pltpu.VMEM(w_out.shape, jnp.bfloat16),
             pltpu.VMEM((rows, width), jnp.float32),
             pltpu.VMEM((rows, hidden), jnp.bfloat16),
+            pltpu.VMEM((width // (2 * HEAD), 2 * rows, 2 * KBLK), jnp.bfloat16),
             pltpu.SemaphoreType.DMA((9,)),
             pltpu.SemaphoreType.DMA((sends,)),
             pltpu.SemaphoreType.DMA((2, gathered[0] // keys.shape[0])),

time: 28.4 us -> 28.2 us (level); the launches traced: 28.3 us -> 27.7 us
  Pallas kernels: 25.9 us -> 25.4 us
    pallas_call x1, Pallas kernels: 25.9 us -> 25.4 us  [fast_shards(): pl.pallas_call(kernel, out_shape=jax.ShapeDtypeStruct((rows, width), jnp....]
where the time goes in v2:
time: 28.2 us; the launch traced here: 27.7 us
  Pallas kernels  25.4 us (90%)
  local copies, waits for them, and re-layouts  1.67 us (6%)
  between operations  0.66 us (2%)
    pallas_call x1, Pallas kernels, fast_shards(): pl.pallas_call(kernel, out_shape=jax.ShapeDtypeStruct((rows, width), jnp....  25.4 us
    unnamed x1, local copies, waits for them, and re-layouts  1.67 us

profile of v2, /device:TPU:1, one launch (start us, length us, event | category | flops | bytes accessed | tf_op | source)
XLA Modules:
  0.0 27.7 jit_solution(17318293241962536347)
XLA Ops:
  0.7 25.4 %shard_map.91 = bf16[128,1024]{1,0:T(8,128)(2,1)} custom-call(s32[1,2]{1,0:T(1,128)} %pattern_hbm.1, s32[1,1]{1,0:T(1,128)} %bitcast.2.counts_hbm, bf16[128,1024]{1,0:T(8,128)(2,1)} %q_hbm.1, bf16[16,1024]{1,0:T(8,128)(2,1)} %k_ref.1, bf16[16,1024]{1,0:T(8,128)(2,1)} %v_ref.1, bf16[128,1024]{1,0:T(8,128)(2,1)} %fine_hbm.1, f32[1,1024]{1,0:T(1,128)} %bitcast.3, ...), custom_call_target="tpu_custom_call" | custom-call | flops 1073741824 | bytes 8388608 | tf_op jit(solution)/shard_map/pallas_call | solution.py:197
  26.0 1.7 %copy.12 = bf16[128,1024]{1,0:T(8,128)(2,1)} copy(bf16[128,1024]{1,0:T(8,128)(2,1)} %shard_map.91) | data formatting | bytes 524288

commit v3 on v2

--- a/solution.py
+++ b/solution.py
@@ -151,16 +151,17 @@
             arrive(kind, origin)
             send(kind, origin, core)
 
-    for kind in (0, 1):
-        for target in z_nbrs:
+    for target in z_nbrs:
+        for kind in (0, 1):
             send(kind, me, target, True)
-    for turn in range(LEVELS + 2):
+    for turn in range(LEVELS + 4):
         if turn < LEVELS:
             column(turn)
-        if 0 <= turn - 1 < LEVELS:
-            beside(turn - 1)
         if 0 <= turn - 2 < LEVELS:
-            across(turn - 2)
+            beside(turn - 2)
+        if 0 <= turn - 4 < LEVELS:
+            across(turn - 4)
+
     def arrive_core(kind):
         for zz in zs:
             for yy in (y, 1 - y):
@@ -174,7 +175,7 @@
     others = [pl.multiple_of(zz * KBLK, KBLK) for zz in zs[1:]]
     second = jnp.broadcast_to(pattern_ref[:, 1:2], (1, 2 * HEAD))
     picks = [jnp.where(second == zz, 1.0, 0.0).astype(jnp.bfloat16) for zz in zs[1:]]
-    used = jnp.broadcast_to(counts_ref[...], (1, KBLK))
+    used = jnp.full((1, KBLK), counts_ref[0], jnp.int32)
     bias = jnp.concatenate([jnp.zeros((1, KBLK), jnp.float32), jnp.where(used > 1, 0.0, -1e30)], axis=1)
     for pair in range(q_ref.shape[1] // (2 * HEAD)):
         weigh_pair(q_ref, kg, weights, own, others, picks, bias, pair)
@@ -201,7 +202,7 @@
         out_specs=vmem,
         scratch_shapes=[
             pltpu.VMEM(pattern.shape, jnp.int32),
-            pltpu.VMEM((1, 1), jnp.int32),
+            pltpu.SMEM(counts.shape, jnp.int32),
             pltpu.VMEM(queries.shape, jnp.bfloat16),
             pltpu.VMEM(fine.shape, jnp.bfloat16),
             pltpu.VMEM((1, width), jnp.float32),
@@ -222,7 +223,7 @@
         cost_estimate=pl.CostEstimate(
             flops=4 * rows * width * hidden, bytes_accessed=4 * width * hidden, transcendentals=rows * hidden
         ),
-    )(pattern, counts.reshape(1, 1), queries, keys, values, fine, norm_gain.reshape(1, -1), w_in, w_out)
+    )(pattern, counts, queries, keys, values, fine, norm_gain.reshape(1, -1), w_in, w_out)
 
 
 def shards(fine, queries, keys, values, pattern, counts, norm_gain, w_in, w_out):

time: 28.2 us -> 27.2 us (0.965); the launches traced: 27.7 us -> 27.1 us
  Pallas kernels: 25.4 us -> 24.8 us
    pallas_call x1, Pallas kernels: 25.4 us -> 24.8 us  [fast_shards(): pl.pallas_call(kernel, out_shape=jax.ShapeDtypeStruct((rows, width), jnp....]
where the time goes in v3:
time: 27.2 us; the launch traced here: 27.1 us
  Pallas kernels  24.8 us (91%)
  local copies, waits for them, and re-layouts  1.67 us (6%)
  between operations  0.66 us (2%)
    pallas_call x1, Pallas kernels, fast_shards(): pl.pallas_call(kernel, out_shape=jax.ShapeDtypeStruct((rows, width), jnp....  24.8 us
    unnamed x1, local copies, waits for them, and re-layouts  1.67 us

profile of v3, /device:TPU:1, one launch (start us, length us, event | category | flops | bytes accessed | tf_op | source)
XLA Modules:
  0.0 27.1 jit_solution(11312941701556427160)
XLA Ops:
  0.7 24.8 %shard_map.91 = bf16[128,1024]{1,0:T(8,128)(2,1)} custom-call(s32[1,2]{1,0:T(1,128)} %pattern_hbm.1, s32[1]{0:T(128)S(6)} %copy.11.counts_hbm, bf16[128,1024]{1,0:T(8,128)(2,1)} %q_hbm.1, bf16[16,1024]{1,0:T(8,128)(2,1)} %k_ref.1, bf16[16,1024]{1,0:T(8,128)(2,1)} %v_ref.1, bf16[128,1024]{1,0:T(8,128)(2,1)} %fine_hbm.1, f32[1,1024]{1,0:T(1,128)} %bitcast.1, ...), custom_call_target="tpu_custom_call" | custom-call | flops 1073741824 | bytes 8388608 | tf_op jit(solution)/shard_map/pallas_call | solution.py:198
  25.4 1.7 %copy.12 = bf16[128,1024]{1,0:T(8,128)(2,1)} copy(bf16[128,1024]{1,0:T(8,128)(2,1)} %shard_map.91) | data formatting | bytes 524288
